TPU v7x, 32 devices: a whole 2x2x4 slice. The times are simulated.
32 devices in a mesh: dp: 8 (over y, x, core), seq: 4 (over z).
Axes of the slice: x: 2, y: 2, z: 4, core: 2. Of those that a mesh axis runs over, the one named last changes fastest.
Arguments:
- query_rows: bfloat16 [4096, 3072], P(('dp', 'seq')), parts along dimension 0, may hold values from -6 to 6
- key_rows: bfloat16 [4096, 3072], P(('dp', 'seq')), parts along dimension 0, may hold values from -6 to 6
- value_rows: bfloat16 [4096, 3072], P(('dp', 'seq')), parts along dimension 0, may hold values from -6 to 6
- query_tangent: bfloat16 [4096, 3072], P(('dp', 'seq')), parts along dimension 0, may hold values from -6 to 6
- key_tangent: bfloat16 [4096, 3072], P(('dp', 'seq')), parts along dimension 0, may hold values from -6 to 6
- value_tangent: bfloat16 [4096, 3072], P(('dp', 'seq')), parts along dimension 0, may hold values from -6 to 6
- cotangent: bfloat16 [4096, 3072], P(('dp', 'seq')), parts along dimension 0, may hold values from -6 to 6
Outputs:
- attended: bfloat16 [4096, 3072], P(('dp', 'seq')), parts along dimension 0
- attended_tangent: bfloat16 [4096, 3072], P(('dp', 'seq')), parts along dimension 0
- grad_query: bfloat16 [4096, 3072], P(('dp', 'seq')), parts along dimension 0
- grad_key: bfloat16 [4096, 3072], P(('dp', 'seq')), parts along dimension 0
- grad_value: bfloat16 [4096, 3072], P(('dp', 'seq')), parts along dimension 0
There are 8 independent parts, one for each index of `dp`. A program takes and returns all parts, laid end to end along the dimension named above; each array names one. Nothing has to cross between parts.
All inputs are finite; a program needn't handle non-finite values.
Results may differ from a plain program's by a relative error of at most 0.0071.
Values may be sent and summed in bfloat16 or wider, within the bound.
A program may use at most 64 MiB of HBM per device.

v0:
```python
import jax
import jax.numpy as jnp
from jax import lax
from jax.sharding import PartitionSpec as P

HEADS = 24
HD = 128


def probabilities(query, keys):
    scale = HD ** (-0.5)
    scores = jnp.dot(query, keys.T, preferred_element_type=jnp.float32) * scale
    top = jnp.max(scores, axis=-1, keepdims=True)
    expo = jnp.exp(scores - top)
    return expo / jnp.sum(expo, axis=-1, keepdims=True)


def forward_head(query, keys, values, query_tan, keys_tan, values_tan):
    scale = HD ** (-0.5)
    probs = probabilities(query, keys)
    probs_half = probs.astype(jnp.bfloat16)
    attended = jnp.dot(probs_half, values, preferred_element_type=jnp.float32).astype(jnp.bfloat16)
    score_tan = (
        jnp.dot(query_tan, keys.T, preferred_element_type=jnp.float32)
        + jnp.dot(query, keys_tan.T, preferred_element_type=jnp.float32)
    ) * scale
    prob_tan = probs * (score_tan - jnp.sum(probs * score_tan, axis=-1, keepdims=True))
    prob_tan = prob_tan.astype(jnp.bfloat16)
    tangent = (
        jnp.dot(prob_tan, values, preferred_element_type=jnp.float32)
        + jnp.dot(probs_half, values_tan, preferred_element_type=jnp.float32)
    ).astype(jnp.bfloat16)
    return (attended, tangent, probs)


def backward_head(probs, query, keys, values, upstream):
    scale = HD ** (-0.5)
    probs_half = probs.astype(jnp.bfloat16)
    grad_values = jnp.dot(probs_half.T, upstream, preferred_element_type=jnp.float32).astype(
        jnp.bfloat16
    )
    prob_grad = jnp.dot(upstream, values.T, preferred_element_type=jnp.float32)
    score_grad = (
        probs * (prob_grad - jnp.sum(probs * prob_grad, axis=-1, keepdims=True)) * scale
    ).astype(jnp.bfloat16)
    grad_q = jnp.dot(score_grad, keys, preferred_element_type=jnp.float32).astype(jnp.bfloat16)
    grad_k = jnp.dot(score_grad.T, query, preferred_element_type=jnp.float32).astype(jnp.bfloat16)
    return (grad_q, grad_k, grad_values)


def take_head(array, index):
    return lax.dynamic_index_in_dim(array, index, 1, keepdims=False)


def put_head(buffer, value, index):
    return lax.dynamic_update_index_in_dim(buffer, value, index, 1)


def body(query_rows, key_rows, value_rows, query_tangent, key_tangent, value_tangent, cotangent):
    tok_rows = query_rows.shape[0]

    def split(array):
        return array.reshape(tok_rows, HEADS, HD)

    query, keys, values, query_tan, keys_tan, values_tan = (
        lax.all_to_all(split(query_rows), "seq", split_axis=1, concat_axis=0, tiled=True),
        lax.all_to_all(split(key_rows), "seq", split_axis=1, concat_axis=0, tiled=True),
        lax.all_to_all(split(value_rows), "seq", split_axis=1, concat_axis=0, tiled=True),
        lax.all_to_all(split(query_tangent), "seq", split_axis=1, concat_axis=0, tiled=True),
        lax.all_to_all(split(key_tangent), "seq", split_axis=1, concat_axis=0, tiled=True),
        lax.all_to_all(split(value_tangent), "seq", split_axis=1, concat_axis=0, tiled=True),
    )
    seq_len = query.shape[0]
    local = query.shape[1]
    stored = jnp.zeros((1, 1, 1), jnp.float32)
    empty = jnp.zeros((seq_len, local, HD), jnp.bfloat16)

    def forward_step(index, carry):
        outs, tans, saved = carry
        attended, tangent, probs = forward_head(
            take_head(query, index),
            take_head(keys, index),
            take_head(values, index),
            take_head(query_tan, index),
            take_head(keys_tan, index),
            take_head(values_tan, index),
        )
        outs = put_head(outs, attended, index)
        tans = put_head(tans, tangent, index)
        return (outs, tans, saved)

    outs, tans, stored = lax.fori_loop(0, local, forward_step, (empty, empty, stored))
    upstream = lax.all_to_all(split(cotangent), "seq", split_axis=1, concat_axis=0, tiled=True)

    def backward_step(index, carry):
        grads_q, grads_k, grads_v = carry
        head_query = take_head(query, index)
        head_keys = take_head(keys, index)
        probs = probabilities(head_query, head_keys)
        grad_q, grad_k, grad_values = backward_head(
            probs, head_query, head_keys, take_head(values, index), take_head(upstream, index)
        )
        return (
            put_head(grads_q, grad_q, index),
            put_head(grads_k, grad_k, index),
            put_head(grads_v, grad_values, index),
        )

    grads_q, grads_k, grads_v = lax.fori_loop(0, local, backward_step, (empty, empty, empty))
    back_out, back_tan, back_q, back_k, back_v = (
        lax.all_to_all(outs, "seq", split_axis=0, concat_axis=1, tiled=True),
        lax.all_to_all(tans, "seq", split_axis=0, concat_axis=1, tiled=True),
        lax.all_to_all(grads_q, "seq", split_axis=0, concat_axis=1, tiled=True),
        lax.all_to_all(grads_k, "seq", split_axis=0, concat_axis=1, tiled=True),
        lax.all_to_all(grads_v, "seq", split_axis=0, concat_axis=1, tiled=True),
    )

    def join(array):
        return array.reshape(tok_rows, HEADS * HD)

    return (join(back_out), join(back_tan), join(back_q), join(back_k), join(back_v))


def solution(mesh):
    in_specs = (
        P(("dp", "seq"), None),
        P(("dp", "seq"), None),
        P(("dp", "seq"), None),
        P(("dp", "seq"), None),
        P(("dp", "seq"), None),
        P(("dp", "seq"), None),
        P(("dp", "seq"), None),
    )
    out_specs = (
        P(("dp", "seq"), None),
        P(("dp", "seq"), None),
        P(("dp", "seq"), None),
        P(("dp", "seq"), None),
        P(("dp", "seq"), None),
    )
    return jax.shard_map(body, mesh=mesh, in_specs=in_specs, out_specs=out_specs, check_vma=False)
```

profile of v0, /device:TPU:0, one launch (start us, length us, event | category | flops | bytes accessed | tf_op | source)
XLA Modules:
  0.0 369.3 jit_solution(3346377999242223430)
XLA Ops:
  0.6 2.3 copy.53
  2.9 6.4 %all-to-all-start = ((bf16[128,24,128]{0,2,1:T(8,128)(2,1)}), bf16[128,24,128]{0,2,1:T(8,128)(2,1)S(1)}, u32[]{:S(2)}, u32[]{:S(2)}) async-start(bf16[128,24,128]{0,2,1:T(8,128)(2,1)} %bitcast.15), calls=%async_computation | async-start | bytes 1572864 | tf_op jit(solution)/shard_map/all_to_all | solution.py:66
  10.5 19.0 %all-to-all-done = bf16[128,24,128]{0,2,1:T(8,128)(2,1)S(1)} async-done(((bf16[128,24,128]{0,2,1:T(8,128)(2,1)}), bf16[128,24,128]{0,2,1:T(8,128)(2,1)S(1)}, u32[]{:S(2)}, u32[]{:S(2)}) %all-to-all-start) | async-done | bytes 786464 | tf_op jit(solution)/shard_map/all_to_all | solution.py:66
  29.5 3.6 all-to-all-start.1
  34.3 18.4 %all-to-all-done.1 = bf16[128,24,128]{0,2,1:T(8,128)(2,1)S(1)} async-done(((bf16[128,24,128]{0,2,1:T(8,128)(2,1)}), bf16[128,24,128]{0,2,1:T(8,128)(2,1)S(1)}, u32[]{:S(2)}, u32[]{:S(2)}) %all-to-all-start.1) | async-done | bytes 786464 | tf_op jit(solution)/shard_map/all_to_all | solution.py:67
  52.7 3.6 all-to-all-start.2
  57.5 18.4 %all-to-all-done.2 = bf16[128,24,128]{0,2,1:T(8,128)(2,1)S(1)} async-done(((bf16[128,24,128]{0,2,1:T(8,128)(2,1)}), bf16[128,24,128]{0,2,1:T(8,128)(2,1)S(1)}, u32[]{:S(2)}, u32[]{:S(2)}) %all-to-all-start.2) | async-done | bytes 786464 | tf_op jit(solution)/shard_map/all_to_all | solution.py:68
  75.9 3.5 all-to-all-start.3
  79.4 2.3 copy.65
  81.7 17.3 %all-to-all-done.3 = bf16[128,24,128]{0,2,1:T(8,128)(2,1)S(1)} async-done(((bf16[128,24,128]{0,2,1:T(8,128)(2,1)}), bf16[128,24,128]{0,2,1:T(8,128)(2,1)S(1)}, u32[]{:S(2)}, u32[]{:S(2)}) %all-to-all-start.3) | async-done | bytes 786464 | tf_op jit(solution)/shard_map/all_to_all | solution.py:69
  99.8 4.2 %all-to-all-start.4 = ((bf16[128,24,128]{0,2,1:T(8,128)(2,1)}), bf16[128,24,128]{0,2,1:T(8,128)(2,1)}, u32[]{:S(2)}, u32[]{:S(2)}) async-start(bf16[128,24,128]{0,2,1:T(8,128)(2,1)} %bitcast.196), calls=%async_computation.4 | async-start | bytes 1572864 | tf_op jit(solution)/shard_map/all_to_all | solution.py:70
  104.0 2.3 copy.68
  106.3 17.4 %all-to-all-done.4 = bf16[128,24,128]{0,2,1:T(8,128)(2,1)} async-done(((bf16[128,24,128]{0,2,1:T(8,128)(2,1)}), bf16[128,24,128]{0,2,1:T(8,128)(2,1)}, u32[]{:S(2)}, u32[]{:S(2)}) %all-to-all-start.4) | async-done | bytes 786464 | tf_op jit(solution)/shard_map/all_to_all | solution.py:70
  123.7 4.3 %all-to-all-start.5 = ((bf16[128,24,128]{0,2,1:T(8,128)(2,1)}), bf16[128,24,128]{0,2,1:T(8,128)(2,1)}, u32[]{:S(2)}, u32[]{:S(2)}) async-start(bf16[128,24,128]{0,2,1:T(8,128)(2,1)} %bitcast.40), calls=%async_computation.5 | async-start | bytes 1572864 | tf_op jit(solution)/shard_map/all_to_all | solution.py:71
  132.3 2.3 copy.67
  134.6 13.1 %all-to-all-done.5 = bf16[128,24,128]{0,2,1:T(8,128)(2,1)} async-done(((bf16[128,24,128]{0,2,1:T(8,128)(2,1)}), bf16[128,24,128]{0,2,1:T(8,128)(2,1)}, u32[]{:S(2)}, u32[]{:S(2)}) %all-to-all-start.5) | async-done | bytes 786464 | tf_op jit(solution)/shard_map/all_to_all | solution.py:71
  147.7 3.5 all-to-all-start.8
  151.2 2.3 copy.70
  155.4 49.6 %while.32 = (s32[]{:T(128)}, bf16[512,6,128]{2,0,1:T(8,128)(2,1)}, bf16[512,6,128]{2,0,1:T(8,128)(2,1)}, bf16[512,6,128]{2,0,1:T(8,128)(2,1)S(1)}, bf16[512,6,12...) while((s32[]{:T(128)}, bf16[512,6,128]{2,0,1:T(8,128)(2,1)}, ...), condition=%wide.region_4.5_spmd, body=%wide.region_0.4_spmd.sunk | while | flops 408353280 | bytes 12483697 | solution.py:92
  156.0 1.9 fusion.107
  161.8 1.9 fusion.110
  164.2 1.9 fusion.107
  170.0 1.9 fusion.110
  172.5 1.9 fusion.107
  178.3 1.9 fusion.110
  180.8 1.9 fusion.107
  186.6 1.9 fusion.110
  189.0 1.9 fusion.107
  194.9 1.9 fusion.110
  197.3 1.9 fusion.107
  203.1 1.9 fusion.110
  205.1 2.7 copy.71
  207.7 5.1 %all-to-all-start.6 = ((bf16[512,6,128]{2,1,0:T(8,128)(2,1)}), bf16[512,6,128]{2,1,0:T(8,128)(2,1)S(1)}, u32[]{:S(2)}, u32[]{:S(2)}) async-start(bf16[512,6,128]{2,1,0:T(8,128)(2,1)} %copy.71), calls=%async_computation.6 | async-start | bytes 2097152 | tf_op jit(solution)/shard_map/all_to_all | solution.py:111
  212.8 2.7 copy.74
  216.6 20.8 %all-to-all-done.6 = bf16[512,6,128]{2,1,0:T(8,128)(2,1)S(1)} async-done(((bf16[512,6,128]{2,1,0:T(8,128)(2,1)}), bf16[512,6,128]{2,1,0:T(8,128)(2,1)S(1)}, u32[]{:S(2)}, u32[]{:S(2)}) %all-to-all-start.6) | async-done | bytes 786464 | tf_op jit(solution)/shard_map/all_to_all | solution.py:111
  237.4 4.2 %all-to-all-start.7 = ((bf16[512,6,128]{2,1,0:T(8,128)(2,1)}), bf16[512,6,128]{2,1,0:T(8,128)(2,1)}, u32[]{:S(2)}, u32[]{:S(2)}) async-start(bf16[512,6,128]{2,1,0:T(8,128)(2,1)} %copy.74), calls=%async_computation.7 | async-start | bytes 2097152 | tf_op jit(solution)/shard_map/all_to_all | solution.py:112
  243.8 32.1 %while.33 = (s32[]{:T(128)}, bf16[512,6,128]{2,0,1:T(8,128)(2,1)S(1)}, bf16[512,6,128]{2,0,1:T(8,128)(2,1)}, bf16[512,6,128]{2,0,1:T(8,128)(2,1)}, bf16[512,6,12...) while((s32[]{:T(128)}, ...), condition=%wide.region_9.10_spmd, body=%wide.region_5.9_spmd.sunk | while | flops 340195840 | bytes 10251365 | solution.py:109
  252.6 1.9 fusion.121
  257.9 1.9 fusion.121
  263.3 1.9 fusion.121
  268.7 1.9 fusion.121
  274.0 1.9 fusion.121
  277.4 5.2 %all-to-all-start.9 = ((bf16[512,6,128]{2,1,0:T(8,128)(2,1)}), bf16[512,6,128]{2,1,0:T(8,128)(2,1)S(1)}, u32[]{:S(2)}, u32[]{:S(2)}) async-start(bf16[512,6,128]{2,1,0:T(8,128)(2,1)} %copy.80), calls=%async_computation.9 | async-start | bytes 2097152 | tf_op jit(solution)/shard_map/all_to_all | solution.py:113
  284.2 23.1 %all-to-all-done.9 = bf16[512,6,128]{2,1,0:T(8,128)(2,1)S(1)} async-done(((bf16[512,6,128]{2,1,0:T(8,128)(2,1)}), bf16[512,6,128]{2,1,0:T(8,128)(2,1)S(1)}, u32[]{:S(2)}, u32[]{:S(2)}) %all-to-all-start.9) | async-done | bytes 786464 | tf_op jit(solution)/shard_map/all_to_all | solution.py:113
  307.3 4.4 %all-to-all-start.10 = ((bf16[512,6,128]{2,1,0:T(8,128)(2,1)}), bf16[512,6,128]{2,1,0:T(8,128)(2,1)}, u32[]{:S(2)}, u32[]{:S(2)}) async-start(bf16[512,6,128]{2,1,0:T(8,128)(2,1)} %copy.83), calls=%async_computation.10 | async-start | bytes 2097152 | tf_op jit(solution)/shard_map/all_to_all | solution.py:114
  313.3 23.7 %all-to-all-done.10 = bf16[512,6,128]{2,1,0:T(8,128)(2,1)} async-done(((bf16[512,6,128]{2,1,0:T(8,128)(2,1)}), bf16[512,6,128]{2,1,0:T(8,128)(2,1)}, u32[]{:S(2)}, u32[]{:S(2)}) %all-to-all-start.10) | async-done | bytes 786464 | tf_op jit(solution)/shard_map/all_to_all | solution.py:114
  337.0 4.2 %all-to-all-start.11 = ((bf16[512,6,128]{2,1,0:T(8,128)(2,1)}), bf16[512,6,128]{2,1,0:T(8,128)(2,1)}, u32[]{:S(2)}, u32[]{:S(2)}) async-start(bf16[512,6,128]{2,1,0:T(8,128)(2,1)} %copy.86), calls=%async_computation.11 | async-start | bytes 2097152 | tf_op jit(solution)/shard_map/all_to_all | solution.py:115
  350.6 16.0 %all-to-all-done.11 = bf16[512,6,128]{2,1,0:T(8,128)(2,1)} async-done(((bf16[512,6,128]{2,1,0:T(8,128)(2,1)}), bf16[512,6,128]{2,1,0:T(8,128)(2,1)}, u32[]{:S(2)}, u32[]{:S(2)}) %all-to-all-start.11) | async-done | bytes 786464 | tf_op jit(solution)/shard_map/all_to_all | solution.py:115
  (112 shorter events, 79.3 us)
Async XLA Ops:
  2.9 6.5 %copy-start.4 = (bf16[128,3072]{1,0:T(8,128)(2,1)S(1)}, bf16[128,3072]{1,0:T(8,128)(2,1)}, u32[]{:S(2)}) copy-start(bf16[128,3072]{1,0:T(8,128)(2,1)} %param.12) | copy-start | bytes 2359300
  2.9 26.6 %all-to-all-start = ((bf16[128,24,128]{0,2,1:T(8,128)(2,1)}), bf16[128,24,128]{0,2,1:T(8,128)(2,1)S(1)}, u32[]{:S(2)}, u32[]{:S(2)}) async-start(bf16[128,24,128]{0,2,1:T(8,128)(2,1)} %bitcast.15), calls=%async_computation | async-start | bytes 1572864 | tf_op jit(solution)/shard_map/all_to_all | solution.py:66
  29.5 3.6 copy-start.5
  29.5 23.2 %all-to-all-start.1 = ((bf16[128,24,128]{0,2,1:T(8,128)(2,1)}), bf16[128,24,128]{0,2,1:T(8,128)(2,1)S(1)}, u32[]{:S(2)}, u32[]{:S(2)}) async-start(bf16[128,24,128]{0,2,1:T(8,128)(2,1)} %bitcast.20), calls=%async_computation.1 | async-start | bytes 1572864 | tf_op jit(solution)/shard_map/all_to_all | solution.py:67
  52.7 3.6 copy-start.6
  52.7 23.2 %all-to-all-start.2 = ((bf16[128,24,128]{0,2,1:T(8,128)(2,1)}), bf16[128,24,128]{0,2,1:T(8,128)(2,1)S(1)}, u32[]{:S(2)}, u32[]{:S(2)}) async-start(bf16[128,24,128]{0,2,1:T(8,128)(2,1)} %bitcast.25), calls=%async_computation.2 | async-start | bytes 1572864 | tf_op jit(solution)/shard_map/all_to_all | solution.py:68
  75.9 23.1 %all-to-all-start.3 = ((bf16[128,24,128]{0,2,1:T(8,128)(2,1)}), bf16[128,24,128]{0,2,1:T(8,128)(2,1)S(1)}, u32[]{:S(2)}, u32[]{:S(2)}) async-start(bf16[128,24,128]{0,2,1:T(8,128)(2,1)} %bitcast.195), calls=%async_computation.3 | async-start | bytes 1572864 | tf_op jit(solution)/shard_map/all_to_all | solution.py:69
  99.0 0.9 copy-start
  99.8 23.8 %all-to-all-start.4 = ((bf16[128,24,128]{0,2,1:T(8,128)(2,1)}), bf16[128,24,128]{0,2,1:T(8,128)(2,1)}, u32[]{:S(2)}, u32[]{:S(2)}) async-start(bf16[128,24,128]{0,2,1:T(8,128)(2,1)} %bitcast.196), calls=%async_computation.4 | async-start | bytes 1572864 | tf_op jit(solution)/shard_map/all_to_all | solution.py:70
  123.7 4.4 %copy-start.7 = (bf16[128,3072]{1,0:T(8,128)(2,1)S(1)}, bf16[128,3072]{1,0:T(8,128)(2,1)}, u32[]{:S(2)}) copy-start(bf16[128,3072]{1,0:T(8,128)(2,1)} %param.17) | copy-start | bytes 2359300
  123.7 24.0 %all-to-all-start.5 = ((bf16[128,24,128]{0,2,1:T(8,128)(2,1)}), bf16[128,24,128]{0,2,1:T(8,128)(2,1)}, u32[]{:S(2)}, u32[]{:S(2)}) async-start(bf16[128,24,128]{0,2,1:T(8,128)(2,1)} %bitcast.40), calls=%async_computation.5 | async-start | bytes 1572864 | tf_op jit(solution)/shard_map/all_to_all | solution.py:71
  130.0 1.2 copy-start.1
  147.7 60.0 %all-to-all-start.8 = ((bf16[128,24,128]{0,2,1:T(8,128)(2,1)}), bf16[128,24,128]{0,2,1:T(8,128)(2,1)S(1)}, u32[]{:S(2)}, u32[]{:S(2)}) async-start(bf16[128,24,128]{0,2,1:T(8,128)(2,1)} %bitcast.53), calls=%async_computation.8 | async-start | bytes 1572864 | tf_op jit(solution)/shard_map/all_to_all | solution.py:93
  207.7 29.7 %all-to-all-start.6 = ((bf16[512,6,128]{2,1,0:T(8,128)(2,1)}), bf16[512,6,128]{2,1,0:T(8,128)(2,1)S(1)}, u32[]{:S(2)}, u32[]{:S(2)}) async-start(bf16[512,6,128]{2,1,0:T(8,128)(2,1)} %copy.71), calls=%async_computation.6 | async-start | bytes 2097152 | tf_op jit(solution)/shard_map/all_to_all | solution.py:111
  237.4 40.0 %all-to-all-start.7 = ((bf16[512,6,128]{2,1,0:T(8,128)(2,1)}), bf16[512,6,128]{2,1,0:T(8,128)(2,1)}, u32[]{:S(2)}, u32[]{:S(2)}) async-start(bf16[512,6,128]{2,1,0:T(8,128)(2,1)} %copy.74), calls=%async_computation.7 | async-start | bytes 2097152 | tf_op jit(solution)/shard_map/all_to_all | solution.py:112
  277.4 5.2 %copy-start.2 = (bf16[512,6,128]{2,0,1:T(8,128)(2,1)S(1)}, bf16[512,6,128]{2,0,1:T(8,128)(2,1)}, u32[]{:S(2)}) copy-start(bf16[512,6,128]{2,0,1:T(8,128)(2,1)} %get-tuple-element.304) | copy-start | bytes 2359300
  277.4 29.8 %all-to-all-start.9 = ((bf16[512,6,128]{2,1,0:T(8,128)(2,1)}), bf16[512,6,128]{2,1,0:T(8,128)(2,1)S(1)}, u32[]{:S(2)}, u32[]{:S(2)}) async-start(bf16[512,6,128]{2,1,0:T(8,128)(2,1)} %copy.80), calls=%async_computation.9 | async-start | bytes 2097152 | tf_op jit(solution)/shard_map/all_to_all | solution.py:113
  284.2 27.6 %copy-start.3 = (bf16[512,6,128]{2,0,1:T(8,128)(2,1)S(1)}, bf16[512,6,128]{2,0,1:T(8,128)(2,1)}, u32[]{:S(2)}) copy-start(bf16[512,6,128]{2,0,1:T(8,128)(2,1)} %get-tuple-element.305) | copy-start | bytes 2359300
  307.3 29.7 %all-to-all-start.10 = ((bf16[512,6,128]{2,1,0:T(8,128)(2,1)}), bf16[512,6,128]{2,1,0:T(8,128)(2,1)}, u32[]{:S(2)}, u32[]{:S(2)}) async-start(bf16[512,6,128]{2,1,0:T(8,128)(2,1)} %copy.83), calls=%async_computation.10 | async-start | bytes 2097152 | tf_op jit(solution)/shard_map/all_to_all | solution.py:114
  337.0 29.5 %all-to-all-start.11 = ((bf16[512,6,128]{2,1,0:T(8,128)(2,1)}), bf16[512,6,128]{2,1,0:T(8,128)(2,1)}, u32[]{:S(2)}, u32[]{:S(2)}) async-start(bf16[512,6,128]{2,1,0:T(8,128)(2,1)} %copy.86), calls=%async_computation.11 | async-start | bytes 2097152 | tf_op jit(solution)/shard_map/all_to_all | solution.py:115
where the time goes:
time: 371 us; the launch traced here: 369 us
  waiting for transfers between devices  187 us (50%)
  matrix products  77.4 us (21%)
  starting transfers between devices  52.4 us (14%)
  local copies, waits for them, and re-layouts  47.2 us (13%)
  other arithmetic  4.11 us (1%)
    all_to_all x1, waiting for transfers between devices, body(): lax.all_to_all(grads_k, 'seq', split_axis=0, concat_axis=1, tiled=True)  23.7 us
    all_to_all x1, waiting for transfers between devices, body(): lax.all_to_all(grads_q, 'seq', split_axis=0, concat_axis=1, tiled=True)  23.1 us
    all_to_all x1, waiting for transfers between devices, body(): lax.all_to_all(outs, 'seq', split_axis=0, concat_axis=1, tiled=True)  20.8 us
    all_to_all x1, waiting for transfers between devices, body(): lax.all_to_all(split(query_rows), 'seq', split_axis=1, concat_axis=0, til...  19 us
    all_to_all x1, waiting for transfers between devices, body(): lax.all_to_all(split(key_rows), 'seq', split_axis=1, concat_axis=0, tiled...  18.4 us
    all_to_all x1, waiting for transfers between devices, body(): lax.all_to_all(split(value_rows), 'seq', split_axis=1, concat_axis=0, til...  18.4 us
    unnamed x28, local copies, waits for them, and re-layouts  18.2 us
    all_to_all x1, waiting for transfers between devices, body(): lax.all_to_all(split(key_tangent), 'seq', split_axis=1, concat_axis=0, ti...  17.4 us
  transfers between devices with their start and end apart: 12, of which 10 were waited for; matrix products, arithmetic and copies ran while one was open for 33% of the time, Pallas kernels for 0%

commit v1 on v0

v1 whole, which is shorter than its diff:
```python
import functools

import jax
import jax.numpy as jnp
from jax import lax
from jax.experimental import pallas as pl
from jax.experimental.pallas import tpu as pltpu
from jax.sharding import PartitionSpec as P

HD = 128
TILE = 256
N_IN = 7
N_OUT = 5


def dot(a, b, contract):
    return lax.dot_general(a, b, (((contract[0],), (contract[1],)), ((), ())), preferred_element_type=jnp.float32)


def attention_tile(query, query_tan, upstream, keys, values, keys_tan, values_tan):
    scale = HD ** (-0.5)
    scores = dot(query, keys, (1, 1)) * scale
    top = jnp.max(scores, axis=-1, keepdims=True)
    expo = jnp.exp(scores - top)
    probs = expo / jnp.sum(expo, axis=-1, keepdims=True)
    probs_half = probs.astype(jnp.bfloat16)
    attended = dot(probs_half, values, (1, 0))
    score_tan = (dot(query_tan, keys, (1, 1)) + dot(query, keys_tan, (1, 1))) * scale
    prob_tan = probs * (score_tan - jnp.sum(probs * score_tan, axis=-1, keepdims=True))
    prob_tan = prob_tan.astype(jnp.bfloat16)
    tangent = dot(prob_tan, values, (1, 0)) + dot(probs_half, values_tan, (1, 0))
    grad_v = dot(probs_half, upstream, (0, 0))
    prob_grad = dot(upstream, values, (1, 1))
    score_grad = probs * (prob_grad - jnp.sum(probs * prob_grad, axis=-1, keepdims=True)) * scale
    score_grad = score_grad.astype(jnp.bfloat16)
    grad_q = dot(score_grad, keys, (1, 0))
    grad_k = dot(score_grad, query, (0, 0))
    return attended, tangent, grad_q, grad_k, grad_v


def kernel(n, local, *refs):
    ins = refs[:N_IN]
    outs = refs[N_IN : N_IN + N_OUT]
    gath, made, in_send, in_recv, out_send, out_recv = refs[N_IN + N_OUT :]
    rows = ins[0].shape[0]
    total = n * rows
    tile = min(TILE, total)
    me = lax.axis_index("seq")

    barrier = pltpu.get_barrier_semaphore()
    for d in range(1, n):
        pl.semaphore_signal(
            barrier, inc=1, device_id={"seq": lax.rem(me + d, n)}, device_id_type=pl.DeviceIdType.MESH
        )
    pl.semaphore_wait(barrier, n - 1)

    mine = pl.ds(pl.multiple_of(me * rows, rows), rows)

    def columns(owner, head):
        return pl.ds(pl.multiple_of((owner * local + head) * HD, HD), HD)

    def send_inputs(head, carry):
        for d in range(1, n):
            peer = lax.rem(me + d, n)
            for a in range(N_IN):
                pltpu.make_async_remote_copy(
                    src_ref=ins[a].at[:, columns(peer, head)],
                    dst_ref=gath.at[head, a, mine, :],
                    send_sem=in_send.at[head],
                    recv_sem=in_recv.at[head],
                    device_id={"seq": peer},
                    device_id_type=pl.DeviceIdType.MESH,
                ).start()
        for a in range(N_IN):
            pltpu.make_async_copy(
                ins[a].at[:, columns(me, head)], gath.at[head, a, mine, :], in_recv.at[head]
            ).start()
        return carry

    lax.fori_loop(0, local, send_inputs, 0)

    def work(head, carry):
        pltpu.make_async_copy(gath.at[head], gath.at[head], in_recv.at[head]).wait()
        keys, values = gath[head, 1], gath[head, 2]
        keys_tan, values_tan = gath[head, 4], gath[head, 5]
        grad_k = grad_v = None
        for t in range(total // tile):
            part = pl.ds(t * tile, tile)
            attended, tangent, grad_q, more_k, more_v = attention_tile(
                gath[head, 0, part, :], gath[head, 3, part, :], gath[head, 6, part, :],
                keys, values, keys_tan, values_tan,
            )
            made[head, 0, part, :] = attended.astype(jnp.bfloat16)
            made[head, 1, part, :] = tangent.astype(jnp.bfloat16)
            made[head, 2, part, :] = grad_q.astype(jnp.bfloat16)
            grad_k = more_k if t == 0 else grad_k + more_k
            grad_v = more_v if t == 0 else grad_v + more_v
        made[head, 3] = grad_k.astype(jnp.bfloat16)
        made[head, 4] = grad_v.astype(jnp.bfloat16)
        for d in range(1, n):
            peer = lax.rem(me + d, n)
            theirs = pl.ds(pl.multiple_of(peer * rows, rows), rows)
            for o in range(N_OUT):
                pltpu.make_async_remote_copy(
                    src_ref=made.at[head, o, theirs, :],
                    dst_ref=outs[o].at[:, columns(me, head)],
                    send_sem=out_send.at[o],
                    recv_sem=out_recv.at[o],
                    device_id={"seq": peer},
                    device_id_type=pl.DeviceIdType.MESH,
                ).start()
        for o in range(N_OUT):
            pltpu.make_async_copy(
                made.at[head, o, mine, :], outs[o].at[:, columns(me, head)], out_recv.at[o]
            ).start()
        return carry

    lax.fori_loop(0, local, work, 0)

    def drain(head, carry):
        sent = gath.at[head, :, pl.ds(0, total - rows), :]
        pltpu.make_async_copy(sent, sent, in_send.at[head]).wait()
        return carry

    lax.fori_loop(0, local, drain, 0)
    for o in range(N_OUT):
        sent = outs[o].at[:, pl.ds(0, (n - 1) * local * HD)]
        pltpu.make_async_copy(sent, sent, out_send.at[o]).wait()
        pltpu.make_async_copy(outs[o], outs[o], out_recv.at[o]).wait()


def solution(mesh):
    n = mesh.shape["seq"]

    def body(*args):
        rows, width = args[0].shape
        local = width // HD // n
        return pl.pallas_call(
            functools.partial(kernel, n, local),
            out_shape=[jax.ShapeDtypeStruct((rows, width), jnp.bfloat16)] * N_OUT,
            in_specs=[pl.BlockSpec(memory_space=pl.ANY)] * N_IN,
            out_specs=[pl.BlockSpec(memory_space=pl.ANY)] * N_OUT,
            scratch_shapes=[
                pltpu.VMEM((local, N_IN, n * rows, HD), jnp.bfloat16),
                pltpu.VMEM((local, N_OUT, n * rows, HD), jnp.bfloat16),
                pltpu.SemaphoreType.DMA((local,)),
                pltpu.SemaphoreType.DMA((local,)),
                pltpu.SemaphoreType.DMA((N_OUT,)),
                pltpu.SemaphoreType.DMA((N_OUT,)),
            ],
            compiler_params=pltpu.CompilerParams(
                collective_id=0, has_side_effects=True, vmem_limit_bytes=48 * 1024 * 1024
            ),
            cost_estimate=pl.CostEstimate(
                flops=20 * local * HD * (n * rows) ** 2,
                bytes_accessed=2 * (N_IN + N_OUT) * rows * width * 2,
                transcendentals=local * (n * rows) ** 2,
            ),
        )(*args)

    spec = P(("dp", "seq"), None)
    return jax.shard_map(
        body, mesh=mesh, in_specs=(spec,) * N_IN, out_specs=(spec,) * N_OUT, check_vma=False
    )
```

time: 371 us -> 214 us (0.58)
  the two profiles are of different devices: /device:TPU:0 before, /device:TPU:9 now
where the time goes in v1:
time: 214 us
  Pallas kernels  206 us (96%)
  local copies, waits for them, and re-layouts  6.66 us (3%)
    pallas_call x1, Pallas kernels, body(): pl.pallas_call(functools.partial(kernel, n, local), out_shape=[jax.ShapeD...  206 us
    unnamed x9, local copies, waits for them, and re-layouts  6.66 us

profile of v1, /device:TPU:9, one launch (start us, length us, event | category | flops | bytes accessed | tf_op | source)
XLA Modules:
  0.0 213.7 jit_solution(477225882577193399)
XLA Ops:
  0.6 0.0 copy-start
  0.6 1.1 copy-done
  1.8 0.0 copy-start.1
  1.8 1.1 copy-done.1
  2.9 206.4 %shard_map.110 = (bf16[128,3072]{1,0:T(8,128)(2,1)S(1)}, bf16[128,3072]{1,0:T(8,128)(2,1)S(1)}, bf16[128,3072]{1,0:T(8,128)(2,1)S(1)}, bf16[128,3072]{1,0:T(8,128)(2,1)S(1)}, bf16[128,3072]{1,0:T(8,128)(2,1)S(1)}) custom-call(bf16[128,3072]{1,0:T(8,128)(2,1)S(1)} %copy-done, bf16[128,3072]{1,0:T(8,128)(2,1)S(1)} %copy-done.1, bf16[128,3072]{1,0:T(8,128)(2,1)} %refs_2_.1, ...), custom_call_target="tpu_custom_call" | custom-call | flops 4026531840 | bytes 18874368 | tf_op jit(solution)/shard_map/pallas_call | solution.py:138
  209.3 0.9 copy.17
  210.2 0.9 copy.18
  211.0 0.9 copy.19
  211.9 0.9 copy.20
  212.8 0.9 copy.21
Async XLA Ops:
  0.6 1.1 copy-start
  1.8 1.1 copy-start.1

commit v2 on v1

--- a/solution.py
+++ b/solution.py
@@ -38,6 +38,30 @@
     return attended, tangent, grad_q, grad_k, grad_v
 
 
+def partners(me, n):
+    if n & (n - 1):
+        return [lax.rem(me + d, n) for d in range(1, n)]
+    order = []
+    for d in list(range(n // 2, n)) + list(range(1, n // 2)):
+        peer = me
+        bit = 1
+        while bit < n:
+            if d & bit:
+                peer = peer + bit - 2 * bit * lax.rem(lax.div(me, bit), 2)
+            bit *= 2
+        order.append(peer)
+    return order
+
+
+def place(*refs):
+    done = refs[2 * N_OUT]
+    copies = [pltpu.make_async_copy(refs[o], refs[N_OUT + o], done.at[o]) for o in range(N_OUT)]
+    for copy in copies:
+        copy.start()
+    for copy in copies:
+        copy.wait()
+
+
 def kernel(n, local, *refs):
     ins = refs[:N_IN]
     outs = refs[N_IN : N_IN + N_OUT]
@@ -47,10 +71,12 @@
     tile = min(TILE, total)
     me = lax.axis_index("seq")
 
+    peers = partners(me, n)
+
     barrier = pltpu.get_barrier_semaphore()
-    for d in range(1, n):
+    for peer in peers:
         pl.semaphore_signal(
-            barrier, inc=1, device_id={"seq": lax.rem(me + d, n)}, device_id_type=pl.DeviceIdType.MESH
+            barrier, inc=1, device_id={"seq": peer}, device_id_type=pl.DeviceIdType.MESH
         )
     pl.semaphore_wait(barrier, n - 1)
 
@@ -60,8 +86,7 @@
         return pl.ds(pl.multiple_of((owner * local + head) * HD, HD), HD)
 
     def send_inputs(head, carry):
-        for d in range(1, n):
-            peer = lax.rem(me + d, n)
+        for peer in peers:
             for a in range(N_IN):
                 pltpu.make_async_remote_copy(
                     src_ref=ins[a].at[:, columns(peer, head)],
@@ -81,6 +106,11 @@
 
     def work(head, carry):
         pltpu.make_async_copy(gath.at[head], gath.at[head], in_recv.at[head]).wait()
+
+        @pl.when(head > 0)
+        def _():
+            send_results(head - 1)
+
         keys, values = gath[head, 1], gath[head, 2]
         keys_tan, values_tan = gath[head, 4], gath[head, 5]
         grad_k = grad_v = None
@@ -97,8 +127,10 @@
             grad_v = more_v if t == 0 else grad_v + more_v
         made[head, 3] = grad_k.astype(jnp.bfloat16)
         made[head, 4] = grad_v.astype(jnp.bfloat16)
-        for d in range(1, n):
-            peer = lax.rem(me + d, n)
+        return carry
+
+    def send_results(head):
+        for peer in peers:
             theirs = pl.ds(pl.multiple_of(peer * rows, rows), rows)
             for o in range(N_OUT):
                 pltpu.make_async_remote_copy(
@@ -113,9 +145,9 @@
             pltpu.make_async_copy(
                 made.at[head, o, mine, :], outs[o].at[:, columns(me, head)], out_recv.at[o]
             ).start()
-        return carry
 
     lax.fori_loop(0, local, work, 0)
+    send_results(local - 1)
 
     def drain(head, carry):
         sent = gath.at[head, :, pl.ds(0, total - rows), :]
@@ -135,9 +167,9 @@
     def body(*args):
         rows, width = args[0].shape
         local = width // HD // n
-        return pl.pallas_call(
+        results = pl.pallas_call(
             functools.partial(kernel, n, local),
-            out_shape=[jax.ShapeDtypeStruct((rows, width), jnp.bfloat16)] * N_OUT,
+            out_shape=[pltpu.VMEM((rows, width), jnp.bfloat16)] * N_OUT,
             in_specs=[pl.BlockSpec(memory_space=pl.ANY)] * N_IN,
             out_specs=[pl.BlockSpec(memory_space=pl.ANY)] * N_OUT,
             scratch_shapes=[
@@ -156,7 +188,16 @@
                 bytes_accessed=2 * (N_IN + N_OUT) * rows * width * 2,
                 transcendentals=local * (n * rows) ** 2,
             ),
-        )(*args)
+        )(*[pltpu.with_memory_space_constraint(x, pltpu.HBM) for x in args])
+        results = [pltpu.with_memory_space_constraint(x, pltpu.VMEM) for x in results]
+        return pl.pallas_call(
+            place,
+            out_shape=[jax.ShapeDtypeStruct((rows, width), jnp.bfloat16)] * N_OUT,
+            in_specs=[pl.BlockSpec(memory_space=pltpu.VMEM)] * N_OUT,
+            out_specs=[pl.BlockSpec(memory_space=pltpu.HBM)] * N_OUT,
+            scratch_shapes=[pltpu.SemaphoreType.DMA((N_OUT,))],
+            compiler_params=pltpu.CompilerParams(vmem_limit_bytes=8 * 1024 * 1024),
+        )(*results)
 
     spec = P(("dp", "seq"), None)
     return jax.shard_map(

time: 214 us -> 209 us (0.977)
  local copies, waits for them, and re-layouts: 6.66 us -> 0 us
  Pallas kernels: 206 us -> 209 us
    unnamed x9 -> x0, local copies, waits for them, and re-layouts: 6.66 us -> none
    pallas_call x1 -> x2, Pallas kernels: 206 us -> 209 us  [the longest x1 207 us: body(): pl.pallas_call(functools.partial(kernel, n, local), out_shape=[pltpu.VMEM...]
where the time goes in v2:
time: 209 us
  Pallas kernels  209 us (100%)
    pallas_call x1, Pallas kernels, body(): pl.pallas_call(functools.partial(kernel, n, local), out_shape=[pltpu.VMEM...  207 us

profile of v2, /device:TPU:9, one launch (start us, length us, event | category | flops | bytes accessed | tf_op | source)
XLA Modules:
  0.0 209.2 jit_solution(13600236452134390530)
XLA Ops:
  0.6 206.6 %shard_map.110 = (bf16[128,3072]{1,0:T(8,128)(2,1)S(1)}, bf16[128,3072]{1,0:T(8,128)(2,1)S(1)}, bf16[128,3072]{1,0:T(8,128)(2,1)S(1)}, bf16[128,3072]{1,0:T(8,128)(2,1)S(1)}, bf16[128,3072]{1,0:T(8,128)(2,1)S(1)}) custom-call(bf16[128,3072]{1,0:T(8,128)(2,1)} %refs_0_.1, bf16[128,3072]{1,0:T(8,128)(2,1)} %refs_1_.1, bf16[128,3072]{1,0:T(8,128)(2,1)} %refs_2_.1, ...), custom_call_target="tpu_custom_call" | custom-call | flops 4026531840 | bytes 18874368 | tf_op jit(solution)/shard_map/pallas_call | solution.py:170
  207.3 2.0 shard_map.111

commit v3 on v2

--- a/solution.py
+++ b/solution.py
@@ -11,6 +11,7 @@
 TILE = 256
 N_IN = 7
 N_OUT = 5
+GROUP = 2
 
 
 def dot(a, b, contract):
@@ -62,12 +63,13 @@
         copy.wait()
 
 
-def kernel(n, local, *refs):
+def kernel(n, local, group, *refs):
     ins = refs[:N_IN]
     outs = refs[N_IN : N_IN + N_OUT]
     gath, made, in_send, in_recv, out_send, out_recv = refs[N_IN + N_OUT :]
     rows = ins[0].shape[0]
     total = n * rows
+    groups, wide = local // group, group * HD
     tile = min(TILE, total)
     me = lax.axis_index("seq")
 
@@ -83,7 +85,7 @@
     mine = pl.ds(pl.multiple_of(me * rows, rows), rows)
 
     def columns(owner, head):
-        return pl.ds(pl.multiple_of((owner * local + head) * HD, HD), HD)
+        return pl.ds(pl.multiple_of((owner * groups + head) * wide, wide), wide)
 
     def send_inputs(head, carry):
         for peer in peers:
@@ -102,7 +104,7 @@
             ).start()
         return carry
 
-    lax.fori_loop(0, local, send_inputs, 0)
+    lax.fori_loop(0, groups, send_inputs, 0)
 
     def work(head, carry):
         pltpu.make_async_copy(gath.at[head], gath.at[head], in_recv.at[head]).wait()
@@ -111,22 +113,24 @@
         def _():
             send_results(head - 1)
 
-        keys, values = gath[head, 1], gath[head, 2]
-        keys_tan, values_tan = gath[head, 4], gath[head, 5]
-        grad_k = grad_v = None
-        for t in range(total // tile):
-            part = pl.ds(t * tile, tile)
-            attended, tangent, grad_q, more_k, more_v = attention_tile(
-                gath[head, 0, part, :], gath[head, 3, part, :], gath[head, 6, part, :],
-                keys, values, keys_tan, values_tan,
-            )
-            made[head, 0, part, :] = attended.astype(jnp.bfloat16)
-            made[head, 1, part, :] = tangent.astype(jnp.bfloat16)
-            made[head, 2, part, :] = grad_q.astype(jnp.bfloat16)
-            grad_k = more_k if t == 0 else grad_k + more_k
-            grad_v = more_v if t == 0 else grad_v + more_v
-        made[head, 3] = grad_k.astype(jnp.bfloat16)
-        made[head, 4] = grad_v.astype(jnp.bfloat16)
+        for h in range(group):
+            one = pl.ds(h * HD, HD)
+            keys, values = gath[head, 1, :, one], gath[head, 2, :, one]
+            keys_tan, values_tan = gath[head, 4, :, one], gath[head, 5, :, one]
+            grad_k = grad_v = None
+            for t in range(total // tile):
+                part = pl.ds(t * tile, tile)
+                attended, tangent, grad_q, more_k, more_v = attention_tile(
+                    gath[head, 0, part, one], gath[head, 3, part, one], gath[head, 6, part, one],
+                    keys, values, keys_tan, values_tan,
+                )
+                made[head, 0, part, one] = attended.astype(jnp.bfloat16)
+                made[head, 1, part, one] = tangent.astype(jnp.bfloat16)
+                made[head, 2, part, one] = grad_q.astype(jnp.bfloat16)
+                grad_k = more_k if t == 0 else grad_k + more_k
+                grad_v = more_v if t == 0 else grad_v + more_v
+            made[head, 3, :, one] = grad_k.astype(jnp.bfloat16)
+            made[head, 4, :, one] = grad_v.astype(jnp.bfloat16)
         return carry
 
     def send_results(head):
@@ -146,17 +150,17 @@
                 made.at[head, o, mine, :], outs[o].at[:, columns(me, head)], out_recv.at[o]
             ).start()
 
-    lax.fori_loop(0, local, work, 0)
-    send_results(local - 1)
+    lax.fori_loop(0, groups, work, 0)
+    send_results(groups - 1)
 
     def drain(head, carry):
         sent = gath.at[head, :, pl.ds(0, total - rows), :]
         pltpu.make_async_copy(sent, sent, in_send.at[head]).wait()
         return carry
 
-    lax.fori_loop(0, local, drain, 0)
+    lax.fori_loop(0, groups, drain, 0)
     for o in range(N_OUT):
-        sent = outs[o].at[:, pl.ds(0, (n - 1) * local * HD)]
+        sent = outs[o].at[:, pl.ds(0, (n - 1) * groups * wide)]
         pltpu.make_async_copy(sent, sent, out_send.at[o]).wait()
         pltpu.make_async_copy(outs[o], outs[o], out_recv.at[o]).wait()
 
@@ -167,16 +171,17 @@
     def body(*args):
         rows, width = args[0].shape
         local = width // HD // n
+        group = GROUP if local % GROUP == 0 else 1
         results = pl.pallas_call(
-            functools.partial(kernel, n, local),
+            functools.partial(kernel, n, local, group),
             out_shape=[pltpu.VMEM((rows, width), jnp.bfloat16)] * N_OUT,
             in_specs=[pl.BlockSpec(memory_space=pl.ANY)] * N_IN,
             out_specs=[pl.BlockSpec(memory_space=pl.ANY)] * N_OUT,
             scratch_shapes=[
-                pltpu.VMEM((local, N_IN, n * rows, HD), jnp.bfloat16),
-                pltpu.VMEM((local, N_OUT, n * rows, HD), jnp.bfloat16),
-                pltpu.SemaphoreType.DMA((local,)),
-                pltpu.SemaphoreType.DMA((local,)),
+                pltpu.VMEM((local // group, N_IN, n * rows, group * HD), jnp.bfloat16),
+                pltpu.VMEM((local // group, N_OUT, n * rows, group * HD), jnp.bfloat16),
+                pltpu.SemaphoreType.DMA((local // group,)),
+                pltpu.SemaphoreType.DMA((local // group,)),
                 pltpu.SemaphoreType.DMA((N_OUT,)),
                 pltpu.SemaphoreType.DMA((N_OUT,)),
             ],

time: 209 us -> 209 us (level)
  no operation moved by 1% of the time
where the time goes in v3:
time: 209 us
  Pallas kernels  208 us (100%)
    pallas_call x1, Pallas kernels, body(): pl.pallas_call(functools.partial(kernel, n, local, group), out_shape=[plt...  206 us

profile of v3, /device:TPU:9, one launch (start us, length us, event | category | flops | bytes accessed | tf_op | source)
XLA Modules:
  0.0 209.1 jit_solution(9018555637362435750)
XLA Ops:
  0.6 206.5 %shard_map.110 = (bf16[128,3072]{1,0:T(8,128)(2,1)S(1)}, bf16[128,3072]{1,0:T(8,128)(2,1)S(1)}, bf16[128,3072]{1,0:T(8,128)(2,1)S(1)}, bf16[128,3072]{1,0:T(8,128)(2,1)S(1)}, bf16[128,3072]{1,0:T(8,128)(2,1)S(1)}) custom-call(bf16[128,3072]{1,0:T(8,128)(2,1)} %refs_0_.1, bf16[128,3072]{1,0:T(8,128)(2,1)} %refs_1_.1, bf16[128,3072]{1,0:T(8,128)(2,1)} %refs_2_.1, ...), custom_call_target="tpu_custom_call" | custom-call | flops 4026531840 | bytes 18874368 | tf_op jit(solution)/shard_map/pallas_call | solution.py:175
  207.1 2.0 shard_map.111
